TPU v7x, 32 devices: a whole 2x2x4 slice. The times are simulated.
32 devices in a mesh: ctx: 8 (over z, y), head: 4 (over x, core).
Axes of the slice: x: 2, y: 2, z: 4, core: 2. Of those that a mesh axis runs over, the one named last changes fastest.
Arguments:
- queries: bfloat16 [4, 2048, 1024], P('head', 'ctx'), may hold values from -6 to 6
- keys: bfloat16 [4, 2048, 128], P('head', 'ctx'), may hold values from -6 to 6
- values: bfloat16 [4, 2048, 128], P('head', 'ctx'), may hold values from -6 to 6
- documents: int32 [4, 2048], P('head', 'ctx'), may hold values from 0 to 3, never falling along the last dimension, each value on 1 to 1024 neighbouring positions
Outputs:
- tokens_out: bfloat16 [4, 2048, 1024], P(None, ('ctx', 'head'))
- log_sums: float32 [4, 8, 2048], P('head', None, 'ctx')
Inputs may be any that keep to these rules, and one draw needn't show every extreme that they name: `documents`: each row's ids never fall along positions; each document holds at most half of the 2048 positions.
All inputs are finite; a program needn't handle non-finite values.
Results may differ from a plain program's by a relative error of at most 0.0075.
Values may be sent and summed in bfloat16 or wider, within the bound.
A program may use at most 64 MiB of HBM per device.

v0:
```python
import jax
import jax.numpy as jnp
from jax import lax
from jax.sharding import PartitionSpec as P

NEG_FILL = -1e30


def attend_block(
    block_state,
    query_rows,
    query_pos,
    query_doc,
    key_rows,
    value_rows,
    key_pos,
    key_doc,
    score_scale,
):
    run_max, run_total, run_acc = block_state
    scores = (
        jnp.einsum("uqgd,ukd->ugqk", query_rows, key_rows, preferred_element_type=jnp.float32)
        * score_scale
    )
    visible = (key_pos[None, None, :] <= query_pos[None, :, None]) & (
        key_doc[:, None, :] == query_doc[:, :, None]
    )
    scores = jnp.where(visible[:, None], scores, NEG_FILL)
    new_max = jnp.maximum(run_max, jnp.max(scores, axis=3))
    weights = jnp.where(visible[:, None], jnp.exp(scores - new_max[..., None]), 0.0)
    factor = jnp.exp(run_max - new_max)
    new_total = factor * run_total + jnp.sum(weights, axis=3)
    rounded = weights.astype(jnp.bfloat16)
    mixed_rows = jnp.einsum(
        "ugqk,ukd->uqgd", rounded, value_rows, preferred_element_type=jnp.float32
    )
    new_acc = jnp.swapaxes(factor, 1, 2)[..., None] * run_acc + mixed_rows
    return (new_max, new_total, new_acc)


def attend_rows(rows, row_docs, row_pos, keys, values, documents):
    unit_count, shard_rows, row_width = rows.shape
    head_dim = keys.shape[2]
    groups = row_width // head_dim
    block_rows = shard_rows // 2
    score_scale = 1.0 / head_dim**0.5
    query_list = []
    pos_list = []
    doc_list = []
    init_list = []
    for block_index in range(2):
        lower = block_index * block_rows
        query_list.append(
            rows[:, lower : lower + block_rows].reshape(unit_count, block_rows, groups, head_dim)
        )
        pos_list.append(row_pos[lower : lower + block_rows])
        doc_list.append(row_docs[:, lower : lower + block_rows])
        init_list.append(
            (
                jnp.full((unit_count, groups, block_rows), NEG_FILL, jnp.float32),
                jnp.zeros((unit_count, groups, block_rows), jnp.float32),
                jnp.zeros((unit_count, block_rows, groups, head_dim), jnp.float32),
            )
        )
    key_all = lax.all_gather(keys, "ctx", axis=1, tiled=True)
    value_all = lax.all_gather(values, "ctx", axis=1, tiled=True)
    doc_all = lax.all_gather(documents, "ctx", axis=1, tiled=True)
    piece_blocks = key_all.shape[1] // shard_rows

    def key_step(step_index, inner_carry):
        offset = step_index * shard_rows
        key_rows = lax.dynamic_slice_in_dim(key_all, offset, shard_rows, 1)
        value_rows = lax.dynamic_slice_in_dim(value_all, offset, shard_rows, 1)
        key_doc = lax.dynamic_slice_in_dim(doc_all, offset, shard_rows, 1)
        key_pos = offset + jnp.arange(shard_rows, dtype=jnp.int32)
        updated = []
        for block_index in range(2):
            query_pos = pos_list[block_index]
            query_doc = doc_list[block_index]
            query_rows = query_list[block_index]
            needed = (key_pos[0] <= query_pos[-1]) & jnp.any(key_doc[:, -1] >= query_doc[:, 0])

            def compute(
                block_state, query_rows=query_rows, query_pos=query_pos, query_doc=query_doc
            ):
                return attend_block(
                    block_state,
                    query_rows,
                    query_pos,
                    query_doc,
                    key_rows,
                    value_rows,
                    key_pos,
                    key_doc,
                    score_scale,
                )

            def keep(block_state):
                return block_state

            updated.append(lax.cond(needed, compute, keep, inner_carry[block_index]))
        return tuple(updated)

    final = lax.fori_loop(0, piece_blocks, key_step, tuple(init_list))
    out_parts = []
    lse_parts = []
    for block_index in range(2):
        run_max, run_total, run_acc = final[block_index]
        normed = (run_acc / jnp.swapaxes(run_total, 1, 2)[..., None]).astype(jnp.bfloat16)
        out_parts.append(normed.reshape(unit_count, block_rows, row_width))
        lse_parts.append(run_max + jnp.log(run_total))
    return (jnp.concatenate(out_parts, axis=1), jnp.concatenate(lse_parts, axis=2))


def body(queries, keys, values, documents):
    my_place = lax.axis_index("ctx")
    shard_rows = queries.shape[1]
    row_pos = my_place * shard_rows + jnp.arange(shard_rows, dtype=jnp.int32)
    own_out, own_lse = attend_rows(queries, documents, row_pos, keys, values, documents)
    tokens_out = lax.all_to_all(own_out, "head", split_axis=1, concat_axis=0, tiled=True)
    return (tokens_out, own_lse)


def solution(mesh):
    in_specs = (
        P("head", "ctx", None),
        P("head", "ctx", None),
        P("head", "ctx", None),
        P("head", "ctx"),
    )
    out_specs = (P(None, ("ctx", "head"), None), P("head", None, "ctx"))
    return jax.shard_map(body, mesh=mesh, in_specs=in_specs, out_specs=out_specs, check_vma=False)
```

profile of v0, /device:TPU:16, one launch (start us, length us, event | category | flops | bytes accessed | tf_op | source)
XLA Modules:
  0.0 166.0 jit_solution(8478739054153314542)
XLA Ops:
  0.6 0.7 copy-done.2
  1.3 15.2 %all_gather.9 = s32[1,2048]{1,0:T(1,128)S(1)} all-gather(s32[1,256]{1,0:T(1,128)S(1)} %copy-done.2), channel_id=1, replica_groups=mesh['ctx'=8,'head'=4] {'ctx'}, dimensions={1}, use_global_device_ids=true | all-gather | bytes 9216 | tf_op jit(solution)/shard_map/all_gather | solution.py:67
  16.5 1.1 fusion.33
  19.0 32.5 %all_gather.10 = bf16[1,2048,128]{2,1,0:T(8,128)(2,1)S(1)} all-gather(bf16[1,256,128]{2,1,0:T(8,128)(2,1)S(1)} %copy-done), channel_id=1, replica_groups=mesh['ctx'=8,'head'=4] {'ctx'}, dimensions={1}, use_global_device_ids=true | all-gather | bytes 589824 | tf_op jit(solution)/shard_map/all_gather | solution.py:65
  51.5 31.4 %all_gather.11 = bf16[1,2048,128]{2,1,0:T(8,128)(2,1)S(1)} all-gather(bf16[1,256,128]{2,1,0:T(8,128)(2,1)S(1)} %copy-done.1), channel_id=1, replica_groups=mesh['ctx'=8,'head'=4] {'ctx'}, dimensions={1}, use_global_device_ids=true | all-gather | bytes 589824 | tf_op jit(solution)/shard_map/all_gather | solution.py:66
  83.1 62.2 %while.23 = (s32[]{:T(128)}, f32[1,8,128]{2,1,0:T(8,128)S(1)}, f32[1,8,128]{2,1,0:T(8,128)S(1)}, f32[1,128,8,128]{3,1,2,0:T(8,128)S(1)}, f32[1,8,128]{2,1,0:T(8,...) while((s32[]{:T(128)}, f32[1,8,128]{2,1,0:T(8,128)S(1)}, ...), condition=%wide.region_9.10_spmd, body=%wide.region_0.9_spmd.sunk | while | flops 273881344 | bytes 9840231 | solution.py:104
  86.8 1.2 conditional.5
  88.0 0.6 slice.78
  90.5 1.2 conditional.4
  95.5 1.2 conditional.5
  96.7 0.6 slice.78
  99.2 1.2 conditional.4
  104.1 1.2 conditional.5
  107.8 1.2 conditional.4
  112.8 1.2 conditional.5
  116.5 1.2 conditional.4
  121.5 1.2 conditional.5
  125.2 1.2 conditional.4
  145.8 1.0 copy.34
  147.3 3.7 %reduce.4 = bf16[256,1024]{1,0:T(8,128)(2,1)S(1)} reduce(bf16[256,1,1024]{2,1,0:T(2,128)(2,1)S(1)} %bitcast.120, bf16[]{:T(256)} %broadcast.144), dimensions={1}, to_apply=%bitcast.93.reduce_sub_computation | reduce | bytes 1048578
  151.0 1.2 reshape.263
  152.2 3.5 %all-to-all-start = ((bf16[4,2,32768]{2,1,0:T(2,128)(2,1)}), bf16[4,2,32768]{2,1,0:T(2,128)(2,1)S(1)}, u32[]{:S(2)}, u32[]{:S(2)}) async-start(bf16[4,2,32768]{2,1,0:T(2,128)(2,1)} %reshape.263), calls=%async_computation | async-start | bytes 1048576 | tf_op jit(solution)/shard_map/all_to_all | solution.py:120
  156.3 8.2 %all-to-all-done = bf16[4,2,32768]{2,1,0:T(2,128)(2,1)S(1)} async-done(((bf16[4,2,32768]{2,1,0:T(2,128)(2,1)}), bf16[4,2,32768]{2,1,0:T(2,128)(2,1)S(1)}, u32[]{:S(2)}, u32[]{:S(2)}) %all-to-all-start) | async-done | bytes 524320 | tf_op jit(solution)/shard_map/all_to_all | solution.py:120
  165.0 1.0 copy.37
  (157 shorter events, 33.1 us)
Async XLA Ops:
  0.6 0.7 copy-start.2
  18.1 0.8 copy-start
  19.0 32.5 %copy-start.1 = (bf16[1,256,128]{2,1,0:T(8,128)(2,1)S(1)}, bf16[1,256,128]{2,1,0:T(8,128)(2,1)}, u32[]{:S(2)}) copy-start(bf16[1,256,128]{2,1,0:T(8,128)(2,1)} %param.12) | copy-start | bytes 196612
  152.2 12.3 %all-to-all-start = ((bf16[4,2,32768]{2,1,0:T(2,128)(2,1)}), bf16[4,2,32768]{2,1,0:T(2,128)(2,1)S(1)}, u32[]{:S(2)}, u32[]{:S(2)}) async-start(bf16[4,2,32768]{2,1,0:T(2,128)(2,1)} %reshape.263), calls=%async_computation | async-start | bytes 1048576 | tf_op jit(solution)/shard_map/all_to_all | solution.py:120
where the time goes:
time: 166 us
  blocking collectives  79.2 us (48%)
  loops' own time  31.5 us (19%)
  local copies, waits for them, and re-layouts  21.9 us (13%)
  other arithmetic  12.9 us (8%)
  waiting for transfers between devices  8.19 us (5%)
  matrix products  7.94 us (5%)
  starting transfers between devices  3.47 us (2%)
    all_gather x1, blocking collectives, attend_rows(): key_all = lax.all_gather(keys, 'ctx', axis=1, tiled=True)  32.5 us
    all_gather x1, blocking collectives, attend_rows(): value_all = lax.all_gather(values, 'ctx', axis=1, tiled=True)  31.4 us
    another operation x1, loops' own time, attend_rows(): final = lax.fori_loop(0, piece_blocks, key_step, tuple(init_list))  30.8 us
    all_gather x1, blocking collectives, attend_rows(): doc_all = lax.all_gather(documents, 'ctx', axis=1, tiled=True)  15.2 us
    slice x16, local copies, waits for them, and re-layouts, key_step(): query_pos[-1]  9.9 us
    all_to_all x1, waiting for transfers between devices, body(): lax.all_to_all(own_out, 'head', split_axis=1, concat_axis=0, tiled=True)  8.19 us
    ge x8, other arithmetic, key_step(): key_doc[:, -1] >= query_doc[:, 0]  4.96 us
    dot_general x10, matrix products, attend_block(): jnp.einsum('ugqk,ukd->uqgd', rounded, value_rows, preferred_element_type=...  4.86 us
  transfers between devices with their start and end apart: 1, of which 1 were waited for; matrix products, arithmetic and copies ran while one was open for 0% of the time, Pallas kernels for 0%

commit v1 on v0

v1 whole, which is shorter than its diff:
```python
import functools
import math

import jax
import jax.numpy as jnp
from jax import lax
from jax.experimental import pallas as pl
from jax.experimental.pallas import tpu as pltpu
from jax.sharding import PartitionSpec as P

MASKED = -1e30
LANES = 128
MESH = pl.DeviceIdType.MESH


def flip(index, mask):
    out = index
    bit = 1
    while bit <= mask:
        if mask & bit:
            out = out + bit * (1 - 2 * (lax.rem(lax.div(index, bit), 2)))
        bit *= 2
    return out


def kernel(
    n_ctx,
    n_head,
    q_hbm,
    k_hbm,
    v_hbm,
    doc_ref,
    out_ref,
    lse_ref,
    q_in,
    q_rows,
    row_doc,
    row_at,
    own_k,
    own_v,
    z_k,
    z_v,
    y_k,
    y_v,
    run_max,
    run_sum,
    run_acc,
    stage,
    lse_cols,
    in_sem,
    z_send,
    z_recv,
    y_send,
    y_recv,
    o_send,
    o_recv,
):
    span = own_v.shape[0]
    head_dim = own_v.shape[1]
    groups = q_in.shape[1] // head_dim
    piece = span // n_head
    pairs, hops = n_ctx // 2, n_ctx // 4
    scale = math.log2(math.e) / math.sqrt(head_dim)

    me = lax.axis_index("ctx")
    head = lax.axis_index("head")
    pair, side = lax.div(me, 2), lax.rem(me, 2)
    partner = me + 1 - 2 * side
    up = lax.rem(me + 2, n_ctx)
    down = lax.rem(me + n_ctx - 2, n_ctx)

    loads = [
        pltpu.make_async_copy(k_hbm, own_k.at[pl.ds(0, span)], in_sem.at[0]),
        pltpu.make_async_copy(v_hbm, own_v, in_sem.at[1]),
        pltpu.make_async_copy(q_hbm, q_in, in_sem.at[2]),
    ]
    for load in loads:
        load.start()
    barrier = pltpu.get_barrier_semaphore()
    for other in (up, down, partner):
        pl.semaphore_signal(barrier, inc=1, device_id={"ctx": other}, device_id_type=MESH)
    for mask in range(1, n_head):
        pl.semaphore_signal(
            barrier, inc=1, device_id={"head": flip(head, mask)}, device_id_type=MESH
        )

    docs = doc_ref[...].astype(jnp.float32)
    tail = own_k.shape[0] - span
    doc_tile = jnp.concatenate(
        [docs[:, at : at + LANES] for at in range(0, span, LANES)]
        + [jnp.zeros((tail - span // LANES, LANES), jnp.float32)],
        axis=0,
    )
    own_k[pl.ds(span, tail), :] = doc_tile.astype(jnp.bfloat16)
    loads[0].wait()
    loads[1].wait()
    pl.semaphore_wait(barrier, 3 + n_head - 1)

    def z_copy(hop, part):
        if part == 0:
            source = own_k if hop == 1 else z_k.at[hop - 2]
            target = z_k.at[hop - 1]
        else:
            source = own_v if hop == 1 else z_v.at[hop - 2]
            target = z_v.at[hop - 1]
        return pltpu.make_async_remote_copy(
            src_ref=source,
            dst_ref=target,
            send_sem=z_send.at[hop - 1, part],
            recv_sem=z_recv.at[hop - 1, part],
            device_id={"ctx": up},
            device_id_type=MESH,
        )

    def y_copy(held, hop, part):
        if part == 0:
            source = own_k if held == 0 else z_k.at[held - 1]
            target = y_k.at[hop - 1]
        else:
            source = own_v if held == 0 else z_v.at[held - 1]
            target = y_v.at[hop - 1]
        return pltpu.make_async_remote_copy(
            src_ref=source,
            dst_ref=target,
            send_sem=y_send.at[hop - 1, part],
            recv_sem=y_recv.at[hop - 1, part],
            device_id={"ctx": partner},
            device_id_type=MESH,
        )

    has_up = pair + 1 < pairs

    def sends(held, part, act):
        if held < hops:

            @pl.when(has_up & (pair >= held))
            def _():
                act(z_copy(held + 1, part))

            @pl.when((side == 0) & (pair >= held))
            def _():
                act(y_copy(held, held + 1, part))

        if held > 0:

            @pl.when((side == 1) & (pair >= held))
            def _():
                act(y_copy(held, held, part))

    for part in range(2):
        sends(0, part, lambda copy: copy.start())

    doc_cols = jnp.transpose(jnp.broadcast_to(docs, (LANES, span)))
    lse_cols[...] = doc_cols
    loads[2].wait()
    for turn in range(n_head):
        dest = flip(head, n_head - 1 - turn)
        rows = pl.ds(pl.multiple_of(dest * piece, piece), piece)
        for group in range(groups):
            q_rows[turn, pl.ds(group * piece, piece), :] = q_in[
                rows, pl.ds(group * head_dim, head_dim)
            ]
        row_doc[turn] = lse_cols[rows, :]
        row_at[turn] = dest * piece + lax.broadcasted_iota(jnp.int32, (piece, LANES), 0)

    def attend(turn, k_ref, v_ref, diagonal):
        key_docs = k_ref[pl.ds(span, tail), :].astype(jnp.float32)
        biases = []
        for at in range(span // LANES):
            seen = row_doc[turn] == key_docs[at : at + 1, :]
            if diagonal:
                key_at = at * LANES + lax.broadcasted_iota(jnp.int32, (piece, LANES), 1)
                seen = seen & (key_at <= row_at[turn])
            biases.append(jnp.where(seen, 0.0, MASKED))
        bias = jnp.concatenate(biases, axis=1)
        scores = lax.dot_general(
            q_rows[turn],
            k_ref[pl.ds(0, span), :],
            (((1,), (1,)), ((), ())),
            preferred_element_type=jnp.float32,
        )
        scores = scores * scale + jnp.concatenate([bias] * groups, axis=0)
        top = jnp.max(scores, axis=1, keepdims=True)
        top = jnp.broadcast_to(top, (groups * piece, LANES))
        if not diagonal:
            old = run_max[turn]
            top = jnp.maximum(top, old)
        weights = [
            jnp.exp2(scores[:, at : at + LANES] - top) for at in range(0, span, LANES)
        ]
        total = functools.reduce(jnp.add, weights)
        mixed = jnp.dot(
            jnp.concatenate([w.astype(jnp.bfloat16) for w in weights], axis=1),
            v_ref[...],
            preferred_element_type=jnp.float32,
        )
        run_max[turn] = top
        if diagonal:
            run_sum[turn] = total
            run_acc[turn] = mixed
        else:
            factor = jnp.exp2(old - top)
            run_sum[turn] = run_sum[turn] * factor + total
            run_acc[turn] = run_acc[turn] * factor + mixed

    def attend_all(k_ref, v_ref, diagonal=False):
        def step(turn, carry):
            attend(turn, k_ref, v_ref, diagonal)
            return carry

        lax.fori_loop(0, n_head, step, 0, unroll=min(4, n_head))

    attend_all(own_k, own_v, True)

    def y_there(hop):
        return pair + side >= hop

    for hop in range(1, hops + 1):

        @pl.when(pair >= hop)
        def _():
            z_copy(hop, 0).wait_recv()

        sends(hop, 0, lambda copy: copy.start())
        if hop > 1:

            @pl.when(y_there(hop - 1))
            def _():
                for part in range(2):
                    y_copy(0, hop - 1, part).wait_recv()
                attend_all(y_k.at[hop - 2], y_v.at[hop - 2])

        @pl.when(pair >= hop)
        def _():
            z_copy(hop, 1).wait_recv()

        sends(hop, 1, lambda copy: copy.start())

        @pl.when(pair >= hop)
        def _():
            attend_all(z_k.at[hop - 1], z_v.at[hop - 1])

    @pl.when(y_there(hops))
    def _():
        for part in range(2):
            y_copy(0, hops, part).wait_recv()

    def out_copy(turn, slot):
        return pltpu.make_async_remote_copy(
            src_ref=stage.at[turn],
            dst_ref=out_ref.at[slot],
            send_sem=o_send.at[turn],
            recv_sem=o_recv.at[turn],
            device_id={"head": flip(head, n_head - 1 - turn)},
            device_id_type=MESH,
        )

    lane = lax.broadcasted_iota(jnp.int32, (piece, LANES), 1)
    for turn in range(n_head):

        @pl.when(y_there(hops))
        def _():
            attend(turn, y_k.at[hops - 1], y_v.at[hops - 1], False)

        dest = flip(head, n_head - 1 - turn)
        total = jnp.sum(run_sum[turn], axis=1, keepdims=True)
        total = jnp.broadcast_to(total, (groups * piece, LANES))
        normed = (run_acc[turn] * (1.0 / total)).astype(jnp.bfloat16)
        for group in range(groups):
            block = normed[group * piece : (group + 1) * piece]
            columns = pl.ds(group * head_dim, head_dim)
            if turn < n_head - 1:
                stage[turn, :, columns] = block
            else:
                out_ref[head, :, columns] = block
        if turn < n_head - 1:
            out_copy(turn, head).start()
        log_sum = run_max[turn] * math.log(2.0) + jnp.log(total)
        columns = jnp.zeros((piece, LANES), jnp.float32)
        for group in range(groups):
            columns = jnp.where(
                lane == group, log_sum[group * piece : (group + 1) * piece], columns
            )
        lse_cols[pl.ds(pl.multiple_of(dest * piece, piece), piece), :] = columns

    lse_ref[...] = jnp.transpose(lse_cols[...])[:groups]

    for held in range(hops + 1):
        for part in range(2):
            sends(held, part, lambda copy: copy.wait_send())
    for turn in range(n_head - 1):
        out_copy(turn, head).wait_send()
    for turn in range(n_head - 1):
        out_copy(turn, flip(head, n_head - 1 - turn)).wait_recv()


def body(n_ctx, n_head, queries, keys, values, documents):
    span, width = queries.shape[1:]
    head_dim = keys.shape[2]
    groups = width // head_dim
    piece, hops, tail = span // n_head, n_ctx // 4, 16
    vmem = pl.BlockSpec(memory_space=pltpu.VMEM)
    hbm = pl.BlockSpec(memory_space=pl.ANY)
    bf16, f32 = jnp.bfloat16, jnp.float32
    stacked = (n_head, groups * piece, LANES)
    out, lse = pl.pallas_call(
        functools.partial(kernel, n_ctx, n_head),
        out_shape=(
            jax.ShapeDtypeStruct((n_head, piece, width), bf16),
            jax.ShapeDtypeStruct((groups, span), f32),
        ),
        in_specs=[hbm, hbm, hbm, vmem],
        out_specs=(vmem, vmem),
        scratch_shapes=[
            pltpu.VMEM((span, width), bf16),
            pltpu.VMEM((n_head, groups * piece, head_dim), bf16),
            pltpu.VMEM((n_head, piece, LANES), f32),
            pltpu.VMEM((n_head, piece, LANES), jnp.int32),
            pltpu.VMEM((span + tail, head_dim), bf16),
            pltpu.VMEM((span, head_dim), bf16),
            pltpu.VMEM((hops, span + tail, head_dim), bf16),
            pltpu.VMEM((hops, span, head_dim), bf16),
            pltpu.VMEM((hops, span + tail, head_dim), bf16),
            pltpu.VMEM((hops, span, head_dim), bf16),
            pltpu.VMEM(stacked, f32),
            pltpu.VMEM(stacked, f32),
            pltpu.VMEM(stacked, f32),
            pltpu.VMEM((n_head, piece, width), bf16),
            pltpu.VMEM((span, LANES), f32),
            pltpu.SemaphoreType.DMA((3,)),
            pltpu.SemaphoreType.DMA((hops, 2)),
            pltpu.SemaphoreType.DMA((hops, 2)),
            pltpu.SemaphoreType.DMA((hops, 2)),
            pltpu.SemaphoreType.DMA((hops, 2)),
            pltpu.SemaphoreType.DMA((n_head,)),
            pltpu.SemaphoreType.DMA((n_head,)),
        ],
        compiler_params=pltpu.CompilerParams(
            collective_id=0, has_side_effects=True, vmem_limit_bytes=40 * 1024 * 1024
        ),
        cost_estimate=pl.CostEstimate(
            flops=2 * 2 * span * width * span * (2 * hops + 1),
            bytes_accessed=4 * span * width,
            transcendentals=span * groups * span * (2 * hops + 1),
        ),
    )(queries[0], keys[0], values[0], documents)
    return out, lse[None]


def solution(mesh):
    n_ctx, n_head = mesh.shape["ctx"], mesh.shape["head"]
    in_specs = (
        P("head", "ctx", None),
        P("head", "ctx", None),
        P("head", "ctx", None),
        P("head", "ctx"),
    )
    out_specs = (P(None, ("ctx", "head"), None), P("head", None, "ctx"))
    return jax.shard_map(
        functools.partial(body, n_ctx, n_head),
        mesh=mesh,
        in_specs=in_specs,
        out_specs=out_specs,
        check_vma=False,
    )
```

time: 166 us -> 26.7 us (0.16)
  blocking collectives: 79.2 us -> 0 us
  loops' own time: 31.5 us -> 0 us
  Pallas kernels: 0 us -> 21 us
  local copies, waits for them, and re-layouts: 21.9 us -> 4.78 us
  other arithmetic: 12.9 us -> 0 us
  waiting for transfers between devices: 8.19 us -> 0 us
  matrix products: 7.94 us -> 0 us
  starting transfers between devices: 3.47 us -> 0 us
    all_gather x3 -> x0, blocking collectives: 79.2 us -> none  [the longest x1 32.5 us: attend_rows(): key_all = lax.all_gather(keys, 'ctx', axis=1, tiled=True)]
    another operation x17 -> x0, loops' own time: 31.5 us -> none  [the longest x1 30.8 us: attend_rows(): final = lax.fori_loop(0, piece_blocks, key_step, tuple(init_list))]
    pallas_call x0 -> x1, Pallas kernels: none -> 21 us  [body(): pl.pallas_call(functools.partial(kernel, n_ctx, n_head), out_shape=(jax.S...]
    slice x27 -> x0, local copies, waits for them, and re-layouts: 15.1 us -> none  [the longest x16 9.9 us: key_step(): query_pos[-1]]
    all_to_all x1 -> x0, waiting for transfers between devices: 8.19 us -> none  [body(): lax.all_to_all(own_out, 'head', split_axis=1, concat_axis=0, tiled=True)]
    dot_general x20 -> x0, matrix products: 7.94 us -> none  [the longest x10 4.86 us: attend_block(): jnp.einsum('ugqk,ukd->uqgd', rounded, value_rows, preferred_element_type=...]
    ge x8 -> x0, other arithmetic: 4.96 us -> none  [key_step(): key_doc[:, -1] >= query_doc[:, 0]]
    unnamed x1 -> x0, other arithmetic: 3.69 us -> none
  transfers between devices with their start and end apart: 1 -> 0, of which waited for: 1 -> 0; matrix products, arithmetic and copies ran while one was open for 0% -> 0% of each run, Pallas kernels for 0% -> 0%
where the time goes in v1:
time: 26.7 us; the launch traced here: 26.5 us
  Pallas kernels  21 us (79%)
  local copies, waits for them, and re-layouts  4.78 us (18%)
  between operations  0.65 us (2%)
    pallas_call x1, Pallas kernels, body(): pl.pallas_call(functools.partial(kernel, n_ctx, n_head), out_shape=(jax.S...  21 us
    unnamed x10, local copies, waits for them, and re-layouts  4.78 us

profile of v1, /device:TPU:16, one launch (start us, length us, event | category | flops | bytes accessed | tf_op | source)
XLA Modules:
  0.0 26.5 jit_solution(10983997151564986551)
XLA Ops:
  0.6 0.0 copy-start.3
  0.6 0.7 %copy-done.3 = s32[1,256]{1,0:T(1,128)S(1)} copy-done((s32[1,256]{1,0:T(1,128)S(1)}, s32[1,256]{1,0:T(1,128)}, u32[]{:S(2)}) %copy-start.3) | copy-done | bytes 1048
  1.3 0.0 copy-start
  1.3 1.0 %copy-done = bf16[1,256,1024]{2,1,0:T(8,128)(2,1)S(1)} copy-done((bf16[1,256,1024]{2,1,0:T(8,128)(2,1)S(1)}, bf16[1,256,1024]{2,1,0:T(8,128)(2,1)}, u32[]{:S(2)}) %copy-start) | copy-done | bytes 524312
  2.4 0.0 copy-start.1
  2.4 0.8 %copy-done.1 = bf16[1,256,128]{2,1,0:T(8,128)(2,1)S(1)} copy-done((bf16[1,256,128]{2,1,0:T(8,128)(2,1)S(1)}, bf16[1,256,128]{2,1,0:T(8,128)(2,1)}, u32[]{:S(2)}) %copy-start.1) | copy-done | bytes 65560
  3.2 0.0 copy-start.2
  3.2 0.8 %copy-done.2 = bf16[1,256,128]{2,1,0:T(8,128)(2,1)S(1)} copy-done((bf16[1,256,128]{2,1,0:T(8,128)(2,1)S(1)}, bf16[1,256,128]{2,1,0:T(8,128)(2,1)}, u32[]{:S(2)}) %copy-start.2) | copy-done | bytes 65560
  4.0 21.0 %shard_map.59 = (bf16[4,64,1024]{2,1,0:T(8,128)(2,1)S(1)}, f32[8,256]{1,0:T(8,128)S(1)}) custom-call(bf16[256,1024]{1,0:T(8,128)(2,1)S(1)} %bitcast.5, bf16[256,128]{1,0:T(8,128)(2,1)S(1)} %bitcast.6, bf16[256,128]{1,0:T(8,128)(2,1)S(1)} %bitcast.7, s32[1,256]{1,0:T(1,128)S(1)} %copy-done.3), custom_call_target="tpu_custom_call" | custom-call | flops 1342177280 | bytes 1048576 | tf_op jit(solution)/shard_map/pallas_call | solution.py:306
  25.1 0.8 %copy.8 = bf16[4,64,1024]{2,1,0:T(8,128)(2,1)} copy(bf16[4,64,1024]{2,1,0:T(8,128)(2,1)S(1)} %get-tuple-element.8) | data formatting | bytes 1048576
  25.9 0.6 %copy.9 = f32[1,8,256]{2,1,0:T(8,128)} copy(f32[1,8,256]{2,1,0:T(8,128)S(1)} %bitcast.4) | data formatting | bytes 16384
Async XLA Ops:
  0.6 0.7 %copy-start.3 = (s32[1,256]{1,0:T(1,128)S(1)}, s32[1,256]{1,0:T(1,128)}, u32[]{:S(2)}) copy-start(s32[1,256]{1,0:T(1,128)} %doc_ref.1) | copy-start | bytes 3076
  1.3 1.0 %copy-start = (bf16[1,256,1024]{2,1,0:T(8,128)(2,1)S(1)}, bf16[1,256,1024]{2,1,0:T(8,128)(2,1)}, u32[]{:S(2)}) copy-start(bf16[1,256,1024]{2,1,0:T(8,128)(2,1)} %param.4) | copy-start | bytes 1572868
  2.4 0.8 %copy-start.1 = (bf16[1,256,128]{2,1,0:T(8,128)(2,1)S(1)}, bf16[1,256,128]{2,1,0:T(8,128)(2,1)}, u32[]{:S(2)}) copy-start(bf16[1,256,128]{2,1,0:T(8,128)(2,1)} %param.5) | copy-start | bytes 196612
  3.2 0.8 %copy-start.2 = (bf16[1,256,128]{2,1,0:T(8,128)(2,1)S(1)}, bf16[1,256,128]{2,1,0:T(8,128)(2,1)}, u32[]{:S(2)}) copy-start(bf16[1,256,128]{2,1,0:T(8,128)(2,1)} %param.6) | copy-start | bytes 196612

commit v2 on v1

--- a/solution.py
+++ b/solution.py
@@ -10,6 +10,7 @@
 
 MASKED = -1e30
 LANES = 128
+VMEM_GRANT = 63 * 1024 * 1024
 MESH = pl.DeviceIdType.MESH
 
 
@@ -29,9 +30,10 @@
     q_hbm,
     k_hbm,
     v_hbm,
-    doc_ref,
+    doc_hbm,
     out_ref,
     lse_ref,
+    doc_ref,
     q_in,
     q_rows,
     row_doc,
@@ -47,6 +49,7 @@
     run_acc,
     stage,
     lse_cols,
+    lse_rows,
     in_sem,
     z_send,
     z_recv,
@@ -66,24 +69,34 @@
     head = lax.axis_index("head")
     pair, side = lax.div(me, 2), lax.rem(me, 2)
     partner = me + 1 - 2 * side
-    up = lax.rem(me + 2, n_ctx)
-    down = lax.rem(me + n_ctx - 2, n_ctx)
+    up, down = me + 2, me - 2
+    has_up, has_down = pair + 1 < pairs, pair > 0
 
     loads = [
         pltpu.make_async_copy(k_hbm, own_k.at[pl.ds(0, span)], in_sem.at[0]),
         pltpu.make_async_copy(v_hbm, own_v, in_sem.at[1]),
-        pltpu.make_async_copy(q_hbm, q_in, in_sem.at[2]),
+        pltpu.make_async_copy(doc_hbm, doc_ref, in_sem.at[2]),
+        pltpu.make_async_copy(q_hbm, q_in, in_sem.at[3]),
     ]
     for load in loads:
         load.start()
     barrier = pltpu.get_barrier_semaphore()
-    for other in (up, down, partner):
-        pl.semaphore_signal(barrier, inc=1, device_id={"ctx": other}, device_id_type=MESH)
+
+    @pl.when(has_up)
+    def _():
+        pl.semaphore_signal(barrier, inc=1, device_id={"ctx": up}, device_id_type=MESH)
+
+    @pl.when(has_down)
+    def _():
+        pl.semaphore_signal(barrier, inc=1, device_id={"ctx": down}, device_id_type=MESH)
+
+    pl.semaphore_signal(barrier, inc=1, device_id={"ctx": partner}, device_id_type=MESH)
     for mask in range(1, n_head):
         pl.semaphore_signal(
             barrier, inc=1, device_id={"head": flip(head, mask)}, device_id_type=MESH
         )
 
+    loads[2].wait()
     docs = doc_ref[...].astype(jnp.float32)
     tail = own_k.shape[0] - span
     doc_tile = jnp.concatenate(
@@ -94,7 +107,7 @@
     own_k[pl.ds(span, tail), :] = doc_tile.astype(jnp.bfloat16)
     loads[0].wait()
     loads[1].wait()
-    pl.semaphore_wait(barrier, 3 + n_head - 1)
+    pl.semaphore_wait(barrier, n_head + has_up.astype(jnp.int32) + has_down.astype(jnp.int32))
 
     def z_copy(hop, part):
         if part == 0:
@@ -128,8 +141,6 @@
             device_id_type=MESH,
         )
 
-    has_up = pair + 1 < pairs
-
     def sends(held, part, act):
         if held < hops:
 
@@ -152,7 +163,7 @@
 
     doc_cols = jnp.transpose(jnp.broadcast_to(docs, (LANES, span)))
     lse_cols[...] = doc_cols
-    loads[2].wait()
+    loads[3].wait()
     for turn in range(n_head):
         dest = flip(head, n_head - 1 - turn)
         rows = pl.ds(pl.multiple_of(dest * piece, piece), piece)
@@ -255,6 +266,8 @@
             device_id_type=MESH,
         )
 
+    own_copy = pltpu.make_async_copy(stage.at[n_head - 1], out_ref.at[head], in_sem.at[0])
+    lse_copy = pltpu.make_async_copy(lse_rows, lse_ref, in_sem.at[1])
     lane = lax.broadcasted_iota(jnp.int32, (piece, LANES), 1)
     for turn in range(n_head):
 
@@ -269,12 +282,11 @@
         for group in range(groups):
             block = normed[group * piece : (group + 1) * piece]
             columns = pl.ds(group * head_dim, head_dim)
-            if turn < n_head - 1:
-                stage[turn, :, columns] = block
-            else:
-                out_ref[head, :, columns] = block
+            stage[turn, :, columns] = block
         if turn < n_head - 1:
             out_copy(turn, head).start()
+        else:
+            own_copy.start()
         log_sum = run_max[turn] * math.log(2.0) + jnp.log(total)
         columns = jnp.zeros((piece, LANES), jnp.float32)
         for group in range(groups):
@@ -283,8 +295,11 @@
             )
         lse_cols[pl.ds(pl.multiple_of(dest * piece, piece), piece), :] = columns
 
-    lse_ref[...] = jnp.transpose(lse_cols[...])[:groups]
-
+    lse_rows[...] = jnp.transpose(lse_cols[...])[:groups]
+    lse_copy.start()
+
+    own_copy.wait()
+    lse_copy.wait()
     for held in range(hops + 1):
         for part in range(2):
             sends(held, part, lambda copy: copy.wait_send())
@@ -294,13 +309,24 @@
         out_copy(turn, flip(head, n_head - 1 - turn)).wait_recv()
 
 
+def hand_over(out_from, lse_from, out_to, lse_to, sem):
+    copies = [
+        pltpu.make_async_copy(out_from.at[at], out_to.at[at], sem.at[at])
+        for at in range(out_from.shape[0])
+    ]
+    copies.append(pltpu.make_async_copy(lse_from, lse_to.at[0], sem.at[len(copies)]))
+    for copy in copies:
+        copy.start()
+    for copy in copies:
+        copy.wait()
+
+
 def body(n_ctx, n_head, queries, keys, values, documents):
     span, width = queries.shape[1:]
     head_dim = keys.shape[2]
     groups = width // head_dim
     piece, hops, tail = span // n_head, n_ctx // 4, 16
-    vmem = pl.BlockSpec(memory_space=pltpu.VMEM)
-    hbm = pl.BlockSpec(memory_space=pl.ANY)
+    hbm = pl.BlockSpec(memory_space=pltpu.HBM)
     bf16, f32 = jnp.bfloat16, jnp.float32
     stacked = (n_head, groups * piece, LANES)
     out, lse = pl.pallas_call(
@@ -309,9 +335,10 @@
             jax.ShapeDtypeStruct((n_head, piece, width), bf16),
             jax.ShapeDtypeStruct((groups, span), f32),
         ),
-        in_specs=[hbm, hbm, hbm, vmem],
-        out_specs=(vmem, vmem),
+        in_specs=[hbm] * 4,
+        out_specs=(hbm, hbm),
         scratch_shapes=[
+            pltpu.VMEM((1, span), jnp.int32),
             pltpu.VMEM((span, width), bf16),
             pltpu.VMEM((n_head, groups * piece, head_dim), bf16),
             pltpu.VMEM((n_head, piece, LANES), f32),
@@ -327,7 +354,8 @@
             pltpu.VMEM(stacked, f32),
             pltpu.VMEM((n_head, piece, width), bf16),
             pltpu.VMEM((span, LANES), f32),
-            pltpu.SemaphoreType.DMA((3,)),
+            pltpu.VMEM((groups, span), f32),
+            pltpu.SemaphoreType.DMA((4,)),
             pltpu.SemaphoreType.DMA((hops, 2)),
             pltpu.SemaphoreType.DMA((hops, 2)),
             pltpu.SemaphoreType.DMA((hops, 2)),
@@ -336,7 +364,7 @@
             pltpu.SemaphoreType.DMA((n_head,)),
         ],
         compiler_params=pltpu.CompilerParams(
-            collective_id=0, has_side_effects=True, vmem_limit_bytes=40 * 1024 * 1024
+            collective_id=0, has_side_effects=True, vmem_limit_bytes=VMEM_GRANT
         ),
         cost_estimate=pl.CostEstimate(
             flops=2 * 2 * span * width * span * (2 * hops + 1),
@@ -344,7 +372,18 @@
             transcendentals=span * groups * span * (2 * hops + 1),
         ),
     )(queries[0], keys[0], values[0], documents)
-    return out, lse[None]
+    out, lse = pl.pallas_call(
+        hand_over,
+        out_shape=(
+            jax.ShapeDtypeStruct((n_head, piece, width), bf16),
+            jax.ShapeDtypeStruct((1, groups, span), f32),
+        ),
+        in_specs=[hbm, hbm],
+        out_specs=(hbm, hbm),
+        scratch_shapes=[pltpu.SemaphoreType.DMA((n_head + 1,))],
+        compiler_params=pltpu.CompilerParams(vmem_limit_bytes=VMEM_GRANT),
+    )(out, lse)
+    return out, lse
 
 
 def solution(mesh):

time: 26.7 us -> 38.2 us (1.43)
  Pallas kernels: 21 us -> 37.4 us
  local copies, waits for them, and re-layouts: 4.78 us -> 0 us
    pallas_call x0 -> x1, Pallas kernels: none -> 17.3 us  [body(): pl.pallas_call(hand_over, out_shape=(jax.ShapeDtypeStruct((n_head, piece,...]
    unnamed x10 -> x0, local copies, waits for them, and re-layouts: 4.78 us -> none
    pallas_call x1, Pallas kernels: 21 us -> 20.1 us  [body(): pl.pallas_call(functools.partial(kernel, n_ctx, n_head), out_shape=(jax.S...]
where the time goes in v2:
time: 38.2 us; the launch traced here: 38 us
  Pallas kernels  37.4 us (98%)
  between operations  0.64 us (2%)
    pallas_call x1, Pallas kernels, body(): pl.pallas_call(functools.partial(kernel, n_ctx, n_head), out_shape=(jax.S...  20.1 us
    pallas_call x1, Pallas kernels, body(): pl.pallas_call(hand_over, out_shape=(jax.ShapeDtypeStruct((n_head, piece,...  17.3 us

profile of v2, /device:TPU:16, one launch (start us, length us, event | category | flops | bytes accessed | tf_op | source)
XLA Modules:
  0.0 38.0 jit_solution(17728203385461611264)
XLA Ops:
  0.6 20.1 %shard_map.59 = (bf16[4,64,1024]{2,1,0:T(8,128)(2,1)}, f32[8,256]{1,0:T(8,128)}) custom-call(bf16[256,1024]{1,0:T(8,128)(2,1)} %bitcast.3, bf16[256,128]{1,0:T(8,128)(2,1)} %bitcast.4, bf16[256,128]{1,0:T(8,128)(2,1)} %bitcast.5, s32[1,256]{1,0:T(1,128)} %doc_hbm.1), custom_call_target="tpu_custom_call" | custom-call | flops 1342177280 | bytes 1048576 | tf_op jit(solution)/shard_map/pallas_call | solution.py:332
  20.7 17.3 %shard_map.60 = (bf16[4,64,1024]{2,1,0:T(8,128)(2,1)}, f32[1,8,256]{2,1,0:T(8,128)}) custom-call(bf16[4,64,1024]{2,1,0:T(8,128)(2,1)} %get-tuple-element.4.out_from, f32[8,256]{1,0:T(8,128)} %get-tuple-element.5.lse_from), custom_call_target="tpu_custom_call" | custom-call | tf_op jit(solution)/shard_map/pallas_call | solution.py:375

commit v3 on v2

--- a/solution.py
+++ b/solution.py
@@ -309,15 +309,23 @@
         out_copy(turn, flip(head, n_head - 1 - turn)).wait_recv()
 
 
-def hand_over(out_from, lse_from, out_to, lse_to, sem):
-    copies = [
-        pltpu.make_async_copy(out_from.at[at], out_to.at[at], sem.at[at])
-        for at in range(out_from.shape[0])
+def hand_over(out_from, lse_from, out_to, lse_to, out_held, lse_held, in_sem, out_sem):
+    count = out_from.shape[0]
+    froms = [out_from.at[at] for at in range(count)] + [lse_from]
+    helds = [out_held.at[at] for at in range(count)] + [lse_held]
+    tos = [out_to.at[at] for at in range(count)] + [lse_to.at[0]]
+    ins = [
+        pltpu.make_async_copy(froms[at], helds[at], in_sem.at[at]) for at in range(count + 1)
     ]
-    copies.append(pltpu.make_async_copy(lse_from, lse_to.at[0], sem.at[len(copies)]))
-    for copy in copies:
+    outs = [
+        pltpu.make_async_copy(helds[at], tos[at], out_sem.at[at]) for at in range(count + 1)
+    ]
+    for copy in ins:
         copy.start()
-    for copy in copies:
+    for at in range(count + 1):
+        ins[at].wait()
+        outs[at].start()
+    for copy in outs:
         copy.wait()
 
 
@@ -380,7 +388,12 @@
         ),
         in_specs=[hbm, hbm],
         out_specs=(hbm, hbm),
-        scratch_shapes=[pltpu.SemaphoreType.DMA((n_head + 1,))],
+        scratch_shapes=[
+            pltpu.VMEM((n_head, piece, width), bf16),
+            pltpu.VMEM((groups, span), f32),
+            pltpu.SemaphoreType.DMA((n_head + 1,)),
+            pltpu.SemaphoreType.DMA((n_head + 1,)),
+        ],
         compiler_params=pltpu.CompilerParams(vmem_limit_bytes=VMEM_GRANT),
     )(out, lse)
     return out, lse

time: 38.2 us -> 22.7 us (0.59)
  Pallas kernels: 37.4 us -> 21.9 us
    pallas_call x1, Pallas kernels: 17.3 us -> 1.84 us  [body(): pl.pallas_call(hand_over, out_shape=(jax.ShapeDtypeStruct((n_head, piece,...]
where the time goes in v3:
time: 22.7 us; the launch traced here: 22.6 us
  Pallas kernels  21.9 us (96%)
  between operations  0.64 us (3%)
    pallas_call x1, Pallas kernels, body(): pl.pallas_call(functools.partial(kernel, n_ctx, n_head), out_shape=(jax.S...  20.1 us
    pallas_call x1, Pallas kernels, body(): pl.pallas_call(hand_over, out_shape=(jax.ShapeDtypeStruct((n_head, piece,...  1.84 us

profile of v3, /device:TPU:16, one launch (start us, length us, event | category | flops | bytes accessed | tf_op | source)
XLA Modules:
  0.0 22.6 jit_solution(4938472229896402261)
XLA Ops:
  0.6 20.1 %shard_map.59 = (bf16[4,64,1024]{2,1,0:T(8,128)(2,1)}, f32[8,256]{1,0:T(8,128)}) custom-call(bf16[256,1024]{1,0:T(8,128)(2,1)} %bitcast.3, bf16[256,128]{1,0:T(8,128)(2,1)} %bitcast.4, bf16[256,128]{1,0:T(8,128)(2,1)} %bitcast.5, s32[1,256]{1,0:T(1,128)} %doc_hbm.1), custom_call_target="tpu_custom_call" | custom-call | flops 1342177280 | bytes 1048576 | tf_op jit(solution)/shard_map/pallas_call | solution.py:340
  20.7 1.8 %shard_map.60 = (bf16[4,64,1024]{2,1,0:T(8,128)(2,1)}, f32[1,8,256]{2,1,0:T(8,128)}) custom-call(bf16[4,64,1024]{2,1,0:T(8,128)(2,1)} %get-tuple-element.4.out_from, f32[8,256]{1,0:T(8,128)} %get-tuple-element.5.lse_from), custom_call_target="tpu_custom_call" | custom-call | tf_op jit(solution)/shard_map/pallas_call | solution.py:383

commit v4 on v3

--- a/solution.py
+++ b/solution.py
@@ -109,16 +109,19 @@
     loads[1].wait()
     pl.semaphore_wait(barrier, n_head + has_up.astype(jnp.int32) + has_down.astype(jnp.int32))
 
+    half = span // 2
+    parts = ((0, half), (half, half + tail), (0, half), (half, half))
+
+    def source_of(held, part):
+        which, rows = part // 2, pl.ds(*parts[part])
+        if held == 0:
+            return (own_k, own_v)[which].at[rows]
+        return (z_k, z_v)[which].at[held - 1, rows]
+
     def z_copy(hop, part):
-        if part == 0:
-            source = own_k if hop == 1 else z_k.at[hop - 2]
-            target = z_k.at[hop - 1]
-        else:
-            source = own_v if hop == 1 else z_v.at[hop - 2]
-            target = z_v.at[hop - 1]
         return pltpu.make_async_remote_copy(
-            src_ref=source,
-            dst_ref=target,
+            src_ref=source_of(hop - 1, part),
+            dst_ref=(z_k, z_v)[part // 2].at[hop - 1, pl.ds(*parts[part])],
             send_sem=z_send.at[hop - 1, part],
             recv_sem=z_recv.at[hop - 1, part],
             device_id={"ctx": up},
@@ -126,15 +129,9 @@
         )
 
     def y_copy(held, hop, part):
-        if part == 0:
-            source = own_k if held == 0 else z_k.at[held - 1]
-            target = y_k.at[hop - 1]
-        else:
-            source = own_v if held == 0 else z_v.at[held - 1]
-            target = y_v.at[hop - 1]
         return pltpu.make_async_remote_copy(
-            src_ref=source,
-            dst_ref=target,
+            src_ref=source_of(held, part),
+            dst_ref=(y_k, y_v)[part // 2].at[hop - 1, pl.ds(*parts[part])],
             send_sem=y_send.at[hop - 1, part],
             recv_sem=y_recv.at[hop - 1, part],
             device_id={"ctx": partner},
@@ -158,7 +155,7 @@
             def _():
                 act(y_copy(held, held, part))
 
-    for part in range(2):
+    for part in range(len(parts)):
         sends(0, part, lambda copy: copy.start())
 
     doc_cols = jnp.transpose(jnp.broadcast_to(docs, (LANES, span)))
@@ -205,56 +202,66 @@
             v_ref[...],
             preferred_element_type=jnp.float32,
         )
-        run_max[turn] = top
         if diagonal:
-            run_sum[turn] = total
-            run_acc[turn] = mixed
-        else:
-            factor = jnp.exp2(old - top)
-            run_sum[turn] = run_sum[turn] * factor + total
-            run_acc[turn] = run_acc[turn] * factor + mixed
-
-    def attend_all(k_ref, v_ref, diagonal=False):
+            return top, total, mixed
+        factor = jnp.exp2(old - top)
+        return top, run_sum[turn] * factor + total, run_acc[turn] * factor + mixed
+
+    def attend_some(first, last, k_ref, v_ref, diagonal=False):
         def step(turn, carry):
-            attend(turn, k_ref, v_ref, diagonal)
+            run_max[turn], run_sum[turn], run_acc[turn] = attend(turn, k_ref, v_ref, diagonal)
             return carry
 
-        lax.fori_loop(0, n_head, step, 0, unroll=min(4, n_head))
-
-    attend_all(own_k, own_v, True)
+        lax.fori_loop(first, last, step, 0, unroll=min(4, last - first))
 
     def y_there(hop):
         return pair + side >= hop
 
-    for hop in range(1, hops + 1):
-
+    middle = n_head // 2
+    spans = ((0, middle), (middle, n_head))
+
+    def own_half(at):
+        attend_some(*spans[at], own_k, own_v, True)
+
+    def z_half(hop, at):
         @pl.when(pair >= hop)
         def _():
-            z_copy(hop, 0).wait_recv()
-
-        sends(hop, 0, lambda copy: copy.start())
-        if hop > 1:
-
-            @pl.when(y_there(hop - 1))
-            def _():
-                for part in range(2):
-                    y_copy(0, hop - 1, part).wait_recv()
-                attend_all(y_k.at[hop - 2], y_v.at[hop - 2])
-
+            attend_some(*spans[at], z_k.at[hop - 1], z_v.at[hop - 1])
+
+    def y_half(hop, at):
+        @pl.when(y_there(hop))
+        def _():
+            if at == 0:
+                y_wait(hop)
+            attend_some(*spans[at], y_k.at[hop - 1], y_v.at[hop - 1])
+
+    def y_wait(hop):
+        for part in range(len(parts)):
+            y_copy(0, hop, part).wait_recv()
+
+    def pass_on(hop, part):
         @pl.when(pair >= hop)
         def _():
-            z_copy(hop, 1).wait_recv()
-
-        sends(hop, 1, lambda copy: copy.start())
-
-        @pl.when(pair >= hop)
-        def _():
-            attend_all(z_k.at[hop - 1], z_v.at[hop - 1])
-
-    @pl.when(y_there(hops))
-    def _():
-        for part in range(2):
-            y_copy(0, hops, part).wait_recv()
+            z_copy(hop, part).wait_recv()
+
+        sends(hop, part, lambda copy: copy.start())
+
+    for hop in range(1, hops + 1):
+        if hop == 1:
+            own_half(0)
+            pass_on(1, 0)
+            own_half(1)
+            for part in range(1, len(parts)):
+                pass_on(1, part)
+        else:
+            for at in range(2):
+                z_half(hop - 1, at)
+                pass_on(hop, at)
+            for at in range(2):
+                y_half(hop - 1, at)
+                pass_on(hop, 2 + at)
+    for at in range(2):
+        z_half(hops, at)
 
     def out_copy(turn, slot):
         return pltpu.make_async_remote_copy(
@@ -268,26 +275,38 @@
 
     own_copy = pltpu.make_async_copy(stage.at[n_head - 1], out_ref.at[head], in_sem.at[0])
     lse_copy = pltpu.make_async_copy(lse_rows, lse_ref, in_sem.at[1])
-    lane = lax.broadcasted_iota(jnp.int32, (piece, LANES), 1)
-    for turn in range(n_head):
-
-        @pl.when(y_there(hops))
-        def _():
-            attend(turn, y_k.at[hops - 1], y_v.at[hops - 1], False)
-
-        dest = flip(head, n_head - 1 - turn)
-        total = jnp.sum(run_sum[turn], axis=1, keepdims=True)
-        total = jnp.broadcast_to(total, (groups * piece, LANES))
-        normed = (run_acc[turn] * (1.0 / total)).astype(jnp.bfloat16)
+    def finish(turn, sums):
+        top, total, mixed = sums
+        total = jnp.broadcast_to(
+            jnp.sum(total, axis=1, keepdims=True), (groups * piece, LANES)
+        )
+        normed = (mixed * (1.0 / total)).astype(jnp.bfloat16)
         for group in range(groups):
-            block = normed[group * piece : (group + 1) * piece]
-            columns = pl.ds(group * head_dim, head_dim)
-            stage[turn, :, columns] = block
+            stage[turn, :, pl.ds(group * head_dim, head_dim)] = normed[
+                group * piece : (group + 1) * piece
+            ]
         if turn < n_head - 1:
             out_copy(turn, head).start()
         else:
             own_copy.start()
-        log_sum = run_max[turn] * math.log(2.0) + jnp.log(total)
+        run_max[turn] = top
+        run_sum[turn] = total
+
+    @pl.when(y_there(hops))
+    def _():
+        y_wait(hops)
+        for turn in range(n_head):
+            finish(turn, attend(turn, y_k.at[hops - 1], y_v.at[hops - 1], False))
+
+    @pl.when(pair + side < hops)
+    def _():
+        for turn in range(n_head):
+            finish(turn, (run_max[turn], run_sum[turn], run_acc[turn]))
+
+    lane = lax.broadcasted_iota(jnp.int32, (piece, LANES), 1)
+    for turn in range(n_head):
+        dest = flip(head, n_head - 1 - turn)
+        log_sum = run_max[turn] * math.log(2.0) + jnp.log(run_sum[turn])
         columns = jnp.zeros((piece, LANES), jnp.float32)
         for group in range(groups):
             columns = jnp.where(
@@ -301,7 +320,7 @@
     own_copy.wait()
     lse_copy.wait()
     for held in range(hops + 1):
-        for part in range(2):
+        for part in range(len(parts)):
             sends(held, part, lambda copy: copy.wait_send())
     for turn in range(n_head - 1):
         out_copy(turn, head).wait_send()
@@ -364,10 +383,10 @@
             pltpu.VMEM((span, LANES), f32),
             pltpu.VMEM((groups, span), f32),
             pltpu.SemaphoreType.DMA((4,)),
-            pltpu.SemaphoreType.DMA((hops, 2)),
-            pltpu.SemaphoreType.DMA((hops, 2)),
-            pltpu.SemaphoreType.DMA((hops, 2)),
-            pltpu.SemaphoreType.DMA((hops, 2)),
+            pltpu.SemaphoreType.DMA((hops, 4)),
+            pltpu.SemaphoreType.DMA((hops, 4)),
+            pltpu.SemaphoreType.DMA((hops, 4)),
+            pltpu.SemaphoreType.DMA((hops, 4)),
             pltpu.SemaphoreType.DMA((n_head,)),
             pltpu.SemaphoreType.DMA((n_head,)),
         ],

time: 22.7 us -> 22.1 us (0.974)
  Pallas kernels: 21.9 us -> 21.3 us
    pallas_call x1, Pallas kernels: 20.1 us -> 19.4 us  [body(): pl.pallas_call(functools.partial(kernel, n_ctx, n_head), out_shape=(jax.S...]
where the time goes in v4:
time: 22.1 us; the launch traced here: 21.9 us
  Pallas kernels  21.3 us (96%)
  between operations  0.64 us (3%)
    pallas_call x1, Pallas kernels, body(): pl.pallas_call(functools.partial(kernel, n_ctx, n_head), out_shape=(jax.S...  19.4 us
    pallas_call x1, Pallas kernels, body(): pl.pallas_call(hand_over, out_shape=(jax.ShapeDtypeStruct((n_head, piece,...  1.84 us

profile of v4, /device:TPU:16, one launch (start us, length us, event | category | flops | bytes accessed | tf_op | source)
XLA Modules:
  0.0 21.9 jit_solution(13354713712035977692)
XLA Ops:
  0.6 19.4 %shard_map.59 = (bf16[4,64,1024]{2,1,0:T(8,128)(2,1)}, f32[8,256]{1,0:T(8,128)}) custom-call(bf16[256,1024]{1,0:T(8,128)(2,1)} %bitcast.3, bf16[256,128]{1,0:T(8,128)(2,1)} %bitcast.4, bf16[256,128]{1,0:T(8,128)(2,1)} %bitcast.5, s32[1,256]{1,0:T(1,128)} %doc_hbm.1), custom_call_target="tpu_custom_call" | custom-call | flops 1342177280 | bytes 1048576 | tf_op jit(solution)/shard_map/pallas_call | solution.py:359
  20.1 1.8 %shard_map.60 = (bf16[4,64,1024]{2,1,0:T(8,128)(2,1)}, f32[1,8,256]{2,1,0:T(8,128)}) custom-call(bf16[4,64,1024]{2,1,0:T(8,128)(2,1)} %get-tuple-element.4.out_from, f32[8,256]{1,0:T(8,128)} %get-tuple-element.5.lse_from), custom_call_target="tpu_custom_call" | custom-call | tf_op jit(solution)/shard_map/pallas_call | solution.py:402

commit v5 on v4

--- a/solution.py
+++ b/solution.py
@@ -47,6 +47,7 @@
     run_max,
     run_sum,
     run_acc,
+    last_weights,
     stage,
     lse_cols,
     lse_rows,
@@ -171,7 +172,7 @@
         row_doc[turn] = lse_cols[rows, :]
         row_at[turn] = dest * piece + lax.broadcasted_iota(jnp.int32, (piece, LANES), 0)
 
-    def attend(turn, k_ref, v_ref, diagonal):
+    def weigh(turn, k_ref, diagonal):
         key_docs = k_ref[pl.ds(span, tail), :].astype(jnp.float32)
         biases = []
         for at in range(span // LANES):
@@ -197,15 +198,19 @@
             jnp.exp2(scores[:, at : at + LANES] - top) for at in range(0, span, LANES)
         ]
         total = functools.reduce(jnp.add, weights)
-        mixed = jnp.dot(
-            jnp.concatenate([w.astype(jnp.bfloat16) for w in weights], axis=1),
-            v_ref[...],
-            preferred_element_type=jnp.float32,
-        )
+        rounded = jnp.concatenate([w.astype(jnp.bfloat16) for w in weights], axis=1)
         if diagonal:
-            return top, total, mixed
+            return top, total, rounded, None
         factor = jnp.exp2(old - top)
-        return top, run_sum[turn] * factor + total, run_acc[turn] * factor + mixed
+        return top, run_sum[turn] * factor + total, rounded, factor
+
+    def mix(rounded, v_ref):
+        return jnp.dot(rounded, v_ref[...], preferred_element_type=jnp.float32)
+
+    def attend(turn, k_ref, v_ref, diagonal):
+        top, total, rounded, factor = weigh(turn, k_ref, diagonal)
+        mixed = mix(rounded, v_ref)
+        return top, total, mixed if diagonal else run_acc[turn] * factor + mixed
 
     def attend_some(first, last, k_ref, v_ref, diagonal=False):
         def step(turn, carry):
@@ -232,11 +237,11 @@
         @pl.when(y_there(hop))
         def _():
             if at == 0:
-                y_wait(hop)
+                y_wait(hop, range(len(parts)))
             attend_some(*spans[at], y_k.at[hop - 1], y_v.at[hop - 1])
 
-    def y_wait(hop):
-        for part in range(len(parts)):
+    def y_wait(hop, some):
+        for part in some:
             y_copy(0, hop, part).wait_recv()
 
     def pass_on(hop, part):
@@ -257,9 +262,19 @@
             for at in range(2):
                 z_half(hop - 1, at)
                 pass_on(hop, at)
-            for at in range(2):
-                y_half(hop - 1, at)
-                pass_on(hop, 2 + at)
+            @pl.when(side == 0)
+            def _():
+                for at in range(2):
+                    y_half(hop - 1, at)
+
+            pass_on(hop, 2)
+            pass_on(hop, 3)
+
+            @pl.when(side == 1)
+            def _():
+                for at in range(2):
+                    y_half(hop - 1, at)
+
     for at in range(2):
         z_half(hops, at)
 
@@ -294,9 +309,16 @@
 
     @pl.when(y_there(hops))
     def _():
-        y_wait(hops)
+        y_wait(hops, (0, 1))
         for turn in range(n_head):
-            finish(turn, attend(turn, y_k.at[hops - 1], y_v.at[hops - 1], False))
+            run_max[turn], run_sum[turn], last_weights[turn], factor = weigh(
+                turn, y_k.at[hops - 1], False
+            )
+            run_acc[turn] = run_acc[turn] * factor
+        y_wait(hops, (2, 3))
+        for turn in range(n_head):
+            mixed = run_acc[turn] + mix(last_weights[turn], y_v.at[hops - 1])
+            finish(turn, (run_max[turn], run_sum[turn], mixed))
 
     @pl.when(pair + side < hops)
     def _():
@@ -379,6 +401,7 @@
             pltpu.VMEM(stacked, f32),
             pltpu.VMEM(stacked, f32),
             pltpu.VMEM(stacked, f32),
+            pltpu.VMEM((n_head, groups * piece, span), bf16),
             pltpu.VMEM((n_head, piece, width), bf16),
             pltpu.VMEM((span, LANES), f32),
             pltpu.VMEM((groups, span), f32),

time: 22.1 us -> 22.4 us (1.014)
  Pallas kernels: 21.3 us -> 21.6 us
    pallas_call x1, Pallas kernels: 19.4 us -> 19.7 us  [body(): pl.pallas_call(functools.partial(kernel, n_ctx, n_head), out_shape=(jax.S...]
where the time goes in v5:
time: 22.4 us; the launch traced here: 22.2 us
  Pallas kernels  21.6 us (96%)
  between operations  0.64 us (3%)
    pallas_call x1, Pallas kernels, body(): pl.pallas_call(functools.partial(kernel, n_ctx, n_head), out_shape=(jax.S...  19.7 us
    pallas_call x1, Pallas kernels, body(): pl.pallas_call(hand_over, out_shape=(jax.ShapeDtypeStruct((n_head, piece,...  1.84 us

profile of v5, /device:TPU:16, one launch (start us, length us, event | category | flops | bytes accessed | tf_op | source)
XLA Modules:
  0.0 22.2 jit_solution(10475653749855700999)
XLA Ops:
  0.6 19.7 %shard_map.59 = (bf16[4,64,1024]{2,1,0:T(8,128)(2,1)}, f32[8,256]{1,0:T(8,128)}) custom-call(bf16[256,1024]{1,0:T(8,128)(2,1)} %bitcast.3, bf16[256,128]{1,0:T(8,128)(2,1)} %bitcast.4, bf16[256,128]{1,0:T(8,128)(2,1)} %bitcast.5, s32[1,256]{1,0:T(1,128)} %doc_hbm.1), custom_call_target="tpu_custom_call" | custom-call | flops 1342177280 | bytes 1048576 | tf_op jit(solution)/shard_map/pallas_call | solution.py:381
  20.4 1.8 %shard_map.60 = (bf16[4,64,1024]{2,1,0:T(8,128)(2,1)}, f32[1,8,256]{2,1,0:T(8,128)}) custom-call(bf16[4,64,1024]{2,1,0:T(8,128)(2,1)} %get-tuple-element.4.out_from, f32[8,256]{1,0:T(8,128)} %get-tuple-element.5.lse_from), custom_call_target="tpu_custom_call" | custom-call | tf_op jit(solution)/shard_map/pallas_call | solution.py:425

commit v6 on v4

--- a/solution.py
+++ b/solution.py
@@ -257,11 +257,11 @@
             for at in range(2):
                 z_half(hop - 1, at)
                 pass_on(hop, at)
-            for at in range(2):
-                y_half(hop - 1, at)
-                pass_on(hop, 2 + at)
-    for at in range(2):
-        z_half(hops, at)
+            y_half(hop - 1, 0)
+            pass_on(hop, 2)
+            if hop < hops:
+                y_half(hop - 1, 1)
+            pass_on(hop, 3)
 
     def out_copy(turn, slot):
         return pltpu.make_async_remote_copy(
@@ -292,16 +292,22 @@
         run_max[turn] = top
         run_sum[turn] = total
 
-    @pl.when(y_there(hops))
-    def _():
-        y_wait(hops)
-        for turn in range(n_head):
-            finish(turn, attend(turn, y_k.at[hops - 1], y_v.at[hops - 1], False))
-
-    @pl.when(pair + side < hops)
-    def _():
-        for turn in range(n_head):
-            finish(turn, (run_max[turn], run_sum[turn], run_acc[turn]))
+    for at in range(2):
+        if at == 1 and hops > 1:
+            y_half(hops - 1, 1)
+        z_half(hops, at)
+
+        @pl.when(y_there(hops))
+        def _():
+            if at == 0:
+                y_wait(hops)
+            for turn in range(*spans[at]):
+                finish(turn, attend(turn, y_k.at[hops - 1], y_v.at[hops - 1], False))
+
+        @pl.when(pair + side < hops)
+        def _():
+            for turn in range(*spans[at]):
+                finish(turn, (run_max[turn], run_sum[turn], run_acc[turn]))
 
     lane = lax.broadcasted_iota(jnp.int32, (piece, LANES), 1)
     for turn in range(n_head):

time: 22.1 us -> 22.1 us (level)
  no operation moved by 1% of the time
where the time goes in v6:
time: 22.1 us; the launch traced here: 21.9 us
  Pallas kernels  21.3 us (96%)
  between operations  0.64 us (3%)
    pallas_call x1, Pallas kernels, body(): pl.pallas_call(functools.partial(kernel, n_ctx, n_head), out_shape=(jax.S...  19.4 us
    pallas_call x1, Pallas kernels, body(): pl.pallas_call(hand_over, out_shape=(jax.ShapeDtypeStruct((n_head, piece,...  1.84 us

profile of v6, /device:TPU:16, one launch (start us, length us, event | category | flops | bytes accessed | tf_op | source)
XLA Modules:
  0.0 21.9 jit_solution(17214855021931333713)
XLA Ops:
  0.6 19.4 %shard_map.59 = (bf16[4,64,1024]{2,1,0:T(8,128)(2,1)}, f32[8,256]{1,0:T(8,128)}) custom-call(bf16[256,1024]{1,0:T(8,128)(2,1)} %bitcast.3, bf16[256,128]{1,0:T(8,128)(2,1)} %bitcast.4, bf16[256,128]{1,0:T(8,128)(2,1)} %bitcast.5, s32[1,256]{1,0:T(1,128)} %doc_hbm.1), custom_call_target="tpu_custom_call" | custom-call | flops 1342177280 | bytes 1048576 | tf_op jit(solution)/shard_map/pallas_call | solution.py:365
  20.1 1.8 %shard_map.60 = (bf16[4,64,1024]{2,1,0:T(8,128)(2,1)}, f32[1,8,256]{2,1,0:T(8,128)}) custom-call(bf16[4,64,1024]{2,1,0:T(8,128)(2,1)} %get-tuple-element.4.out_from, f32[8,256]{1,0:T(8,128)} %get-tuple-element.5.lse_from), custom_call_target="tpu_custom_call" | custom-call | tf_op jit(solution)/shard_map/pallas_call | solution.py:408
